TPU v7x, 32 devices: a whole 2x2x4 slice. The times are simulated.
32 devices in a mesh: rep: 2 (over y), clu: 8 (over z, x), sub: 2 (over core).
Axes of the slice: x: 2, y: 2, z: 4, core: 2. Of those that a mesh axis runs over, the one named last changes fastest.
Arguments:
- electronegativity: float32 [128, 256], P(('rep', 'clu'), 'sub'), parts along dimension 0, may hold values from -6 to 6
- mm_potential: float32 [128, 256], P(('rep', 'clu'), 'sub'), parts along dimension 0, may hold values from -12 to 12
- hardness: float32 [128, 256], P(('rep', 'clu'), 'sub'), parts along dimension 0, may hold values from 4 to 10
- near_blocks: bfloat16 [128, 3, 256, 256], P(('rep', 'clu'), None, 'sub'), parts along dimension 0, as said below
- near_source: int32 [128, 3], P(('rep', 'clu')), parts along dimension 0, may hold values from 0 to 63, as said below
- basis_in: bfloat16 [128, 32, 256], P(('rep', 'clu'), None, 'sub'), parts along dimension 0, may hold values from -0.375 to 0.375
- far_coupling: bfloat16 [16, 8, 4, 1024], P(('rep', 'clu')), parts along dimension 0
- far_source: int32 [16, 8, 4], P(('rep', 'clu')), parts along dimension 0, may hold values from 0 to 7, as said below
- far_target: int32 [16, 8, 4], P(('rep', 'clu')), parts along dimension 0, may hold values from 0 to 7
- far_count: int32 [16, 8], P(('rep', 'clu')), parts along dimension 0, may hold values from 0 to 4, as said below
Outputs:
- charges: float32 [128, 256], P(('rep', 'clu'), 'sub'), parts along dimension 0
- residual: float32 [128, 256], P(('rep', 'clu'), 'sub'), parts along dimension 0
There are 2 independent parts, one for each index of `rep`. A program takes and returns all parts, laid end to end along the dimension named above; each array names one. Nothing has to cross between parts.
Inputs may be any that keep to these rules, and one draw needn't show every extreme that they name: `near_source`: entry 0 of each cluster's list is the cluster itself; the other two entries are, in either order, the clusters 8 above and 8 below it, replaced by the cluster itself where that one does not exist. `near_blocks`: the near operator is symmetric: the block of cluster c for source s is the transpose of the block of s for source c, and the sum of a cluster's blocks whose source is itself is symmetric. Slots at or past the count are unused; far_count is symmetric, zero from an owner to itself, and every row of receiving owners has some sending owner using all 4 slots. `far_source`: slot k from s to d is the mirror of slot k from d to s: source and target are swapped and the coupling matrix is transposed.
All inputs are finite; a program needn't handle non-finite values.
Results may differ from a plain program's by a relative error of at most 0.00055.
Values sent between devices are 32-bit elements; how exact they have to be, the bound alone decides.
A program may use at most 64 MiB of HBM per device.

v0:
```python
import jax
import jax.numpy as jnp
from jax import lax
from jax.sharding import PartitionSpec as P

ITERS = 3


HIGHEST = lax.Precision.HIGHEST


def with_halo(array, sides, width):
    for axis, dim in sides:
        size, length = (lax.axis_size(axis), array.shape[dim])
        up = [(i, (i + 1) % size) for i in range(size - 1)]
        down = [(j, i) for i, j in up]
        last = lax.slice_in_dim(array, length - width, length, axis=dim)
        leading = lax.slice_in_dim(array, 0, width, axis=dim)
        before = lax.ppermute(last, axis, up)
        after = lax.ppermute(leading, axis, down)
        array = jnp.concatenate([before, array, after], axis=dim)
    return array


def shards(
    electronegativity,
    mm_potential,
    hardness,
    near_blocks,
    near_source,
    basis_in,
    far_coupling,
    far_source,
    far_target,
    far_count,
):
    clusters = hardness.shape[0]
    owners = far_coupling.shape[1]
    slot_cap = far_coupling.shape[2]
    rank_size = basis_in.shape[1]
    first_cluster = lax.axis_index("clu") * clusters
    near_local = near_source - (first_cluster - clusters)
    coupling = far_coupling[0].reshape(owners, slot_cap, rank_size, rank_size).astype(jnp.float32)
    bases_in = basis_in.astype(jnp.float32)
    live_slots = (jnp.arange(slot_cap, dtype=jnp.int32)[None, :] < far_count[0][:, None]).astype(
        jnp.float32
    )
    targets = jax.nn.one_hot(far_target[0], clusters, dtype=jnp.float32)
    source_local = far_source[0]
    global_source = jnp.arange(owners, dtype=jnp.int32)[:, None] * clusters + source_local
    right = -(electronegativity + mm_potential)
    charges = jnp.zeros_like(right)
    residual = right
    direction = right
    norm_now = lax.psum(jnp.sum(residual * residual), ("clu", "sub"))
    for iteration in range(ITERS):
        gathered_rows = lax.all_gather(direction, "sub", axis=1, tiled=True)
        widened = with_halo(gathered_rows, (("clu", 0),), clusters)
        picked = jnp.take(widened, near_local, axis=0)
        near_term = jnp.einsum(
            "cnab,cnb->ca", near_blocks.astype(jnp.float32), picked, precision=HIGHEST
        )
        partial_coeffs = jnp.einsum("crb,cb->cr", bases_in, direction, precision=HIGHEST)
        apply_coeffs = lax.psum(partial_coeffs, "sub")
        piece = lax.all_gather(apply_coeffs, "clu", axis=0, tiled=True)
        inside = (global_source >= 0) & (global_source < piece.shape[0])
        fetched = jnp.take(piece, jnp.clip(global_source, 0, piece.shape[0] - 1), axis=0)
        slot_coeffs = jnp.where(inside[..., None], fetched, 0.0)
        moved_terms = (
            jnp.einsum("skab,skb->ska", coupling, slot_coeffs, precision=HIGHEST)
            * live_slots[..., None]
        )
        target_sums = jnp.einsum("skc,ska->ca", targets, moved_terms, precision=HIGHEST)
        far_term = jnp.einsum("ca,cab->cb", target_sums, bases_in, precision=HIGHEST)
        product_vec = hardness * direction + near_term + far_term
        curvature = lax.psum(jnp.sum(direction * product_vec), ("clu", "sub"))
        step_size = norm_now / curvature
        charges = charges + step_size * direction
        residual = residual - step_size * product_vec
        norm_next = lax.psum(jnp.sum(residual * residual), ("clu", "sub"))
        direction = residual + norm_next / norm_now * direction
        norm_now = norm_next
    return (charges, residual)


def solution(mesh):
    placed = (
        P(("rep", "clu"), "sub"),
        P(("rep", "clu"), "sub"),
        P(("rep", "clu"), "sub"),
        P(("rep", "clu"), None, "sub", None),
        P(("rep", "clu"), None),
        P(("rep", "clu"), None, "sub"),
        P(("rep", "clu"), None, None, None),
        P(("rep", "clu"), None, None),
        P(("rep", "clu"), None, None),
        P(("rep", "clu"), None),
    )
    return jax.shard_map(
        shards,
        mesh=mesh,
        in_specs=placed,
        out_specs=(P(("rep", "clu"), "sub"), P(("rep", "clu"), "sub")),
        check_vma=False,
    )
```

profile of v0, /device:TPU:0, one launch (start us, length us, event | category | flops | bytes accessed | tf_op | source)
XLA Modules:
  0.0 298.6 jit_solution(2875354541202713412)
XLA Ops:
  0.6 1.4 multiply_reduce_fusion.5
  2.1 1.9 all_gather.18
  4.0 4.7 %collective-permute-start = (f32[8,256]{1,0:T(8,128)S(1)}, f32[8,256]{1,0:T(8,128)S(1)}, u32[]{:S(2)}, u32[]{:S(2)}) collective-permute-start(f32[8,256]{1,0:T(8,128)S(1)} %all_gather.18), channel_id=1, source_target_pairs={{0,2},{2,4},{4,6},{6,8},{8,10},{10,12},{12,14},{1,3},{3,5},{5,7},{... | collective-permute-start | bytes 24584 | tf_op jit(solution)/shard_map/ppermute | solution.py:19
  8.7 1.3 collective-permute-start.1
  10.0 0.7 compare_and_fusion.1
  10.9 1.0 fusion.19
  11.9 2.5 psum.64
  14.4 32.8 %all_gather.19 = f32[64,32]{1,0:T(8,128)S(1)} all-gather(f32[8,32]{1,0:T(8,128)S(1)} %psum.64), channel_id=1, replica_groups=mesh['rep'=2,'clu'=8,'sub'=2] {'clu'}, dimensions={0}, use_global_device_ids=true | all-gather | bytes 9216 | tf_op jit(solution)/shard_map/all_gather | solution.py:65
  47.2 0.7 compare_and_fusion
  48.2 1.1 reshape_squeeze.3
  49.3 0.8 copy.28
  50.1 0.7 fusion.18
  52.2 1.0 fusion.21
  54.1 1.3 fusion.4
  56.0 30.1 %all-reduce = (f32[]{:T(128)}, f32[]{:T(128)}) all-reduce(f32[]{:T(128)} %get-tuple-element.14, f32[]{:T(128)} %multiply_reduce_fusion.4), channel_id=1, replica_groups=mesh['rep'=2,'clu'=8,'sub'=2] {'clu','sub'}, use_global_device_ids=true, to_apply=%region_1.2 | all-reduce | flops 2 | bytes 16 | tf_op jit(solution)/shard_map/psum | solution.py:55
  88.1 30.1 %psum.66 = f32[]{:T(128)} all-reduce(f32[]{:T(128)} %get-tuple-element.8), channel_id=1, replica_groups=mesh['rep'=2,'clu'=8,'sub'=2] {'clu','sub'}, use_global_device_ids=true, to_apply=%region_6.9 | all-reduce | flops 1 | bytes 8 | tf_op jit(solution)/shard_map/psum | solution.py:80
  119.5 1.8 all_gather.20
  121.3 1.3 collective-permute-start.2
  122.6 1.3 collective-permute-start.3
  124.1 2.5 psum.67
  126.6 30.4 %all_gather.21 = f32[64,32]{1,0:T(8,128)S(1)} all-gather(f32[8,32]{1,0:T(8,128)S(1)} %psum.67), channel_id=1, replica_groups=mesh['rep'=2,'clu'=8,'sub'=2] {'clu'}, dimensions={0}, use_global_device_ids=true | all-gather | bytes 9216 | tf_op jit(solution)/shard_map/all_gather | solution.py:65
  159.3 1.3 fusion.2
  160.6 0.6 multiply_reduce_fusion.2
  161.3 30.1 %psum.68 = f32[]{:T(128)} all-reduce(f32[]{:T(128)} %multiply_reduce_fusion.2), channel_id=1, replica_groups=mesh['rep'=2,'clu'=8,'sub'=2] {'clu','sub'}, use_global_device_ids=true, to_apply=%region_9.12 | all-reduce | flops 1 | bytes 8 | tf_op jit(solution)/shard_map/psum | solution.py:76
  193.3 30.1 %psum.69 = f32[]{:T(128)} all-reduce(f32[]{:T(128)} %get-tuple-element.6), channel_id=1, replica_groups=mesh['rep'=2,'clu'=8,'sub'=2] {'clu','sub'}, use_global_device_ids=true, to_apply=%region_11.14 | all-reduce | flops 1 | bytes 8 | tf_op jit(solution)/shard_map/psum | solution.py:80
  224.8 1.8 all_gather.22
  226.6 1.3 collective-permute-start.4
  227.9 1.3 collective-permute-start.5
  229.4 2.5 psum.70
  231.8 30.4 %all_gather.23 = f32[64,32]{1,0:T(8,128)S(1)} all-gather(f32[8,32]{1,0:T(8,128)S(1)} %psum.70), channel_id=1, replica_groups=mesh['rep'=2,'clu'=8,'sub'=2] {'clu'}, dimensions={0}, use_global_device_ids=true | all-gather | bytes 9216 | tf_op jit(solution)/shard_map/all_gather | solution.py:65
  264.6 1.3 fusion
  266.5 30.1 %psum.71 = f32[]{:T(128)} all-reduce(f32[]{:T(128)} %multiply_reduce_fusion), channel_id=1, replica_groups=mesh['rep'=2,'clu'=8,'sub'=2] {'clu','sub'}, use_global_device_ids=true, to_apply=%region_14.17 | all-reduce | flops 1 | bytes 8 | tf_op jit(solution)/shard_map/psum | solution.py:76
  (57 shorter events, 10.9 us)
Async XLA Ops:
  0.6 53.4 %copy-start = (bf16[8,3,128,256]{3,2,1,0:T(8,128)(2,1)S(1)}, bf16[8,3,128,256]{3,2,1,0:T(8,128)(2,1)}, u32[]{:S(2)}) copy-start(bf16[8,3,128,256]{3,2,1,0:T(8,128)(2,1)} %param.17) | copy-start | bytes 4718596
  4.0 49.4 %collective-permute-start = (f32[8,256]{1,0:T(8,128)S(1)}, f32[8,256]{1,0:T(8,128)S(1)}, u32[]{:S(2)}, u32[]{:S(2)}) collective-permute-start(f32[8,256]{1,0:T(8,128)S(1)} %all_gather.18), channel_id=1, source_target_pairs={{0,2},{2,4},{4,6},{6,8},{8,10},{10,12},{12,14},{1,3},{3,5},{5,7},{... | collective-permute-start | bytes 24584 | tf_op jit(solution)/shard_map/ppermute | solution.py:19
  8.7 44.7 %collective-permute-start.1 = (f32[8,256]{1,0:T(8,128)S(1)}, f32[8,256]{1,0:T(8,128)S(1)}, u32[]{:S(2)}, u32[]{:S(2)}) collective-permute-start(f32[8,256]{1,0:T(8,128)S(1)} %all_gather.18), channel_id=1, source_target_pairs={{2,0},{4,2},{6,4},{8,6},{10,8},{12,10},{14,12},{3,1},{5,3},{7,5},{... | collective-permute-start | bytes 24584 | tf_op jit(solution)/shard_map/ppermute | solution.py:20
  48.0 7.4 %copy-start.1 = (f32[8,128]{1,0:T(8,128)S(1)}, f32[8,128]{1,0:T(8,128)}, u32[]{:S(2)}) copy-start(f32[8,128]{1,0:T(8,128)} %param.16) | copy-start | bytes 12292
  48.2 75.7 %copy-start.2 = (bf16[8,32,128]{2,1,0:T(8,128)(2,1)S(1)}, bf16[8,32,128]{2,1,0:T(8,128)(2,1)}, u32[]{:S(2)}) copy-start(bf16[8,32,128]{2,1,0:T(8,128)(2,1)} %param.19) | copy-start | bytes 196612
  121.3 37.3 %collective-permute-start.2 = (f32[8,256]{1,0:T(8,128)S(1)}, f32[8,256]{1,0:T(8,128)S(1)}, u32[]{:S(2)}, u32[]{:S(2)}) collective-permute-start(f32[8,256]{1,0:T(8,128)S(1)} %all_gather.20), channel_id=1, source_target_pairs={{0,2},{2,4},{4,6},{6,8},{8,10},{10,12},{12,14},{1,3},{3,5},{5,7},{... | collective-permute-start | bytes 24584 | tf_op jit(solution)/shard_map/ppermute | solution.py:19
  122.6 36.0 %collective-permute-start.3 = (f32[8,256]{1,0:T(8,128)S(1)}, f32[8,256]{1,0:T(8,128)S(1)}, u32[]{:S(2)}, u32[]{:S(2)}) collective-permute-start(f32[8,256]{1,0:T(8,128)S(1)} %all_gather.20), channel_id=1, source_target_pairs={{2,0},{4,2},{6,4},{8,6},{10,8},{12,10},{14,12},{3,1},{5,3},{7,5},{... | collective-permute-start | bytes 24584 | tf_op jit(solution)/shard_map/ppermute | solution.py:20
  226.6 37.3 %collective-permute-start.4 = (f32[8,256]{1,0:T(8,128)S(1)}, f32[8,256]{1,0:T(8,128)S(1)}, u32[]{:S(2)}, u32[]{:S(2)}) collective-permute-start(f32[8,256]{1,0:T(8,128)S(1)} %all_gather.22), channel_id=1, source_target_pairs={{0,2},{2,4},{4,6},{6,8},{8,10},{10,12},{12,14},{1,3},{3,5},{5,7},{... | collective-permute-start | bytes 24584 | tf_op jit(solution)/shard_map/ppermute | solution.py:19
  227.9 36.0 %collective-permute-start.5 = (f32[8,256]{1,0:T(8,128)S(1)}, f32[8,256]{1,0:T(8,128)S(1)}, u32[]{:S(2)}, u32[]{:S(2)}) collective-permute-start(f32[8,256]{1,0:T(8,128)S(1)} %all_gather.22), channel_id=1, source_target_pairs={{2,0},{4,2},{6,4},{8,6},{10,8},{12,10},{14,12},{3,1},{5,3},{7,5},{... | collective-permute-start | bytes 24584 | tf_op jit(solution)/shard_map/ppermute | solution.py:20
where the time goes:
time: 299 us
  blocking collectives  257 us (86%)
  starting transfers between devices  11.1 us (4%)
  matrix products  9.11 us (3%)
  other arithmetic  7.74 us (3%)
  between operations  7.56 us (3%)
  local copies, waits for them, and re-layouts  5.99 us (2%)
    all_gather x3, blocking collectives, shards(): piece = lax.all_gather(apply_coeffs, 'clu', axis=0, tiled=True)  93.6 us
    psum x2, blocking collectives, shards(): norm_next = lax.psum(jnp.sum(residual * residual), ('clu', 'sub'))  60.2 us
    psum x2, blocking collectives, shards(): curvature = lax.psum(jnp.sum(direction * product_vec), ('clu', 'sub'))  60.2 us
    psum x1, blocking collectives, shards(): norm_now = lax.psum(jnp.sum(residual * residual), ('clu', 'sub'))  30.1 us
    psum x3, blocking collectives, shards(): apply_coeffs = lax.psum(partial_coeffs, 'sub')  7.42 us
    ppermute x3, starting transfers between devices, with_halo(): before = lax.ppermute(last, axis, up)  7.24 us
  transfers between devices with their start and end apart: 6, of which 0 were waited for; matrix products, arithmetic and copies ran while one was open for 4% of the time, Pallas kernels for 0%

commit v1 on v0

v1 whole, which is shorter than its diff:
```python
import functools

import jax
import jax.numpy as jnp
from jax import lax
from jax.experimental import pallas as pl
from jax.experimental.pallas import tpu as pltpu
from jax.sharding import PartitionSpec as P

ITERS = 3
MESH = pl.DeviceIdType.MESH
F32 = jnp.float32
BF16 = jnp.bfloat16
SELF, ABOVE, BELOW = 0, 1, 2


def each(first, count, body):
    if count - first <= 8:
        for i in range(first, count):
            body(i)
    else:
        lax.fori_loop(first, count, lambda i, _: (body(i), 0)[1], 0)


def halves(x):
    high = x.astype(BF16)
    low = (x - high.astype(F32)).astype(BF16)
    return high, low


def contract(a, b, dims):
    return lax.dot_general(a, b, (dims, ((), ())), preferred_element_type=F32)


def kernel(
    owners,
    electro,
    potential,
    hardness_ref,
    near_hbm,
    near_source,
    basis,
    coupling,
    target,
    count,
    charges_out,
    residual_out,
    near,
    picked_basis,
    expand,
    mask,
    fields,
    outbox,
    inbox,
    load_sem,
    field_send,
    field_recv,
    slab_send,
    slab_recv,
):
    clusters, atoms = hardness_ref.shape
    slots = target.shape[2]
    rank = basis.shape[1]
    width = slots * rank
    group = 8
    groups = owners // group
    span = group * width
    peers = 2 * owners - 1
    clu = lax.axis_index("clu")
    sub = lax.axis_index("sub")
    mine = 2 * clu + sub

    def to_peers(act):
        def owner_step(o):
            d = lax.rem(clu + o, owners)
            act(d, 0)
            act(d, 1)

        act(clu, 1 - sub)
        each(1, owners, owner_step)

    barrier = pltpu.get_barrier_semaphore()
    to_peers(
        lambda d, t: pl.semaphore_signal(
            barrier, inc=1, device_id={"clu": d, "sub": t}, device_id_type=MESH
        )
    )
    load = pltpu.make_async_copy(near_hbm, near, load_sem)
    load.start()

    row8 = lax.broadcasted_iota(jnp.int32, (clusters, 128), 0)
    slot_of_lane = lax.broadcasted_iota(jnp.int32, (clusters, width), 1) // rank

    def prepare(s):
        wanted = jnp.full((clusters, width), -1, jnp.int32)
        for k in range(slots):
            t = target[0, s, k]
            picked_basis[pl.ds((s * slots + k) * rank, rank), :] = basis[t]
            wanted = jnp.where(slot_of_lane == k, t, wanted)
        hit = (wanted == lax.broadcasted_iota(jnp.int32, (clusters, width), 0)) & (
            slot_of_lane < count[0, s]
        )
        mask[s] = jnp.where(hit, 1.0, 0.0)

    each(0, owners, prepare)

    def send_field(rnd, v):
        fields[rnd, SELF, sub] = v
        source = fields.at[rnd, SELF, sub]

        def copy(kind, d, t):
            pltpu.make_async_remote_copy(
                src_ref=source,
                dst_ref=fields.at[rnd, kind, sub],
                send_sem=field_send.at[rnd, kind],
                recv_sem=field_recv.at[rnd, kind],
                device_id={"clu": d, "sub": t},
                device_id_type=MESH,
            ).start()

        copy(SELF, clu, 1 - sub)

        @pl.when(clu < owners - 1)
        def _():
            copy(BELOW, clu + 1, 0)
            copy(BELOW, clu + 1, 1)

        @pl.when(clu > 0)
        def _():
            copy(ABOVE, clu - 1, 0)
            copy(ABOVE, clu - 1, 1)

    def send_slabs(rnd, sums):
        def copy(d, t):
            pltpu.make_async_remote_copy(
                src_ref=outbox.at[rnd, d],
                dst_ref=inbox.at[rnd, mine],
                send_sem=slab_send.at[rnd],
                recv_sem=slab_recv.at[rnd],
                device_id={"clu": d, "sub": t},
                device_id_type=MESH,
            ).start()

        to_peers(copy)
        inbox[rnd, mine] = sums

    def send_far(rnd, v, sums):
        parts = jnp.concatenate(halves(v), axis=0)

        def group_step(g):
            wide = contract(
                parts, picked_basis[pl.ds(pl.multiple_of(g * span, span), span), :], ((1,), (1,))
            )
            for j in range(group):
                piece = wide[:, j * width : (j + 1) * width]
                piece = (piece[:clusters] + piece[clusters:]) * mask[g * group + j]
                line = jnp.sum(piece, axis=0, keepdims=True)
                outbox[rnd, g * group + j] = jnp.where(row8 == 0, line, sums)

        each(0, groups, group_step)
        send_slabs(rnd, jnp.where(row8 == 0, 0.0, sums))

    def send_sums(rnd, sums):
        each(0, owners, lambda d: outbox.__setitem__((rnd, d), sums))
        send_slabs(rnd, sums)

    def wait_all(ref, sem):
        pltpu.make_async_copy(ref, ref, sem).wait()

    def near_term(rnd):
        wait_all(fields.at[rnd, SELF, 0], field_recv.at[rnd, SELF])

        @pl.when(clu < owners - 1)
        def _():
            wait_all(fields.at[rnd, ABOVE], field_recv.at[rnd, ABOVE])

        @pl.when(clu > 0)
        def _():
            wait_all(fields.at[rnd, BELOW], field_recv.at[rnd, BELOW])

        def whole(kind):
            return jnp.concatenate([fields[rnd, kind, 0], fields[rnd, kind, 1]], axis=1)

        own, above, below = (whole(SELF), whole(ABOVE), whole(BELOW))
        here = clu * clusters + lax.broadcasted_iota(jnp.int32, (clusters, 1), 0)
        inputs = []
        for n in range(near.shape[1]):
            if n == 0:
                value = own
            else:
                origin = near_source[:, n : n + 1]
                value = jnp.where(
                    origin == here + clusters,
                    above,
                    jnp.where(origin == here - clusters, below, own),
                )
            inputs.append(jnp.concatenate(halves(value), axis=0))
        owner_row = lax.broadcasted_iota(jnp.int32, inputs[0].shape, 0) % clusters
        total = None
        blocks = [(c, n) for c in range(clusters) for n in range(near.shape[1])]
        for first, second in zip(blocks[::2], blocks[1::2]):
            left = jnp.concatenate(
                [
                    jnp.where(owner_row == c, inputs[n], jnp.zeros_like(inputs[n]))
                    for c, n in (first, second)
                ],
                axis=0,
            )
            right = jnp.concatenate([near[c, n] for c, n in (first, second)], axis=0)
            product = contract(left, right, ((1,), (1,)))
            total = product if total is None else total + product
        size = 2 * clusters
        first, second = (total[:size, :atoms], total[size:, atoms:])
        both = first + second
        return both[:clusters] + both[clusters:]

    def receive(rnd):
        wait_all(inbox.at[rnd, pl.ds(0, peers)], slab_recv.at[rnd])

    def far_term(rnd):
        def group_step(g):
            lefts = []
            for j in range(group):
                s = g * group + j
                line = inbox[rnd, 2 * s, 0:1, :] + inbox[rnd, 2 * s + 1, 0:1, :]
                lefts.append(line * mask[s])
            left = jnp.concatenate(lefts, axis=1)
            left = jnp.concatenate(halves(left), axis=0)
            right = expand[pl.ds(pl.multiple_of(g * span, span), span), :]
            out = contract(left, right, ((1,), (0,)))
            out = out[:clusters] + out[clusters:]
            return out[:, :atoms] + out[:, atoms:]

        if groups == 1:
            return group_step(0)
        return lax.fori_loop(
            0, groups, lambda g, acc: acc + group_step(g), jnp.zeros((clusters, atoms), F32)
        )

    def totals(rnd):
        if owners <= 8:
            values = [inbox[rnd, i] for i in range(2 * owners)]
            while len(values) > 1:
                values = [a + b for a, b in zip(values[::2], values[1::2])]
            all_sums = values[0]
        else:
            all_sums = lax.fori_loop(
                0, 2 * owners, lambda i, acc: acc + inbox[rnd, i], jnp.zeros((8, 128), F32)
            )
        lane_sum = jnp.sum(all_sums, axis=1, keepdims=True)
        return [lane_sum[i : i + 1, :] for i in range(1, 5)]

    def pack(*pairs):
        out = jnp.zeros((8, 128), F32)
        for i, (a, b) in enumerate(pairs):
            out = jnp.where(row8 == i + 1, jnp.sum(a * b, axis=0, keepdims=True), out)
        return out

    def build_expand():
        row = lax.broadcasted_iota(jnp.int32, (width, width), 0)
        lane = lax.broadcasted_iota(jnp.int32, (width, width), 1)
        spread = jnp.where(row % rank == lane % rank, 1.0, 0.0).astype(BF16)
        per_chunk = width // rank
        same = row // rank == lane // rank

        def step(s):
            lines = coupling[0, s].astype(F32)
            folded = jnp.zeros((width, width), F32)
            for j in range(rank * rank // width):
                chunk = lines[:, j * width : (j + 1) * width]
                tall = jnp.broadcast_to(chunk[:, None, :], (slots, rank, width)).reshape(
                    width, width
                )
                folded = jnp.where(row % rank == lane // rank + j * per_chunk, tall, folded)
            tiled = contract(folded.astype(BF16), spread, ((1,), (0,)))
            diagonal = jnp.where(same, tiled, 0.0).astype(BF16)
            place = pl.ds(pl.multiple_of(s * width, width), width)
            high, low = halves(contract(diagonal, picked_basis[place, :], ((0,), (0,))))
            expand[place, 0:atoms] = high
            expand[place, atoms : 2 * atoms] = low

        each(0, owners, step)

    hardness = hardness_ref[...]
    r = -(electro[...] + potential[...])
    x = jnp.zeros_like(r)
    empty = jnp.zeros((8, 128), F32)
    pl.semaphore_wait(barrier, peers)

    send_field(0, r)
    send_far(0, r, empty)
    build_expand()
    load.wait()
    w = hardness * r + near_term(0)
    receive(0)
    w = w + far_term(0)

    p, s, z, rr, curvature, step = (None,) * 6
    for i in range(ITERS):
        rnd = i + 1
        if i == 0:
            sums = pack((r, r), (r, w))
        else:
            sums = pack((r, r), (r, w), (r, s), (p, w))
        last = i == ITERS - 1
        if last:
            send_sums(rnd, sums)
            receive(rnd)
        else:
            send_field(rnd, w)
            send_far(rnd, w, sums)
            q = hardness * w + near_term(rnd)
            receive(rnd)
        new, rw, rs, pw = totals(rnd)
        if not last:
            q = q + far_term(rnd)
        if i == 0:
            curvature = rw
            p, s = (r, w)
            z = q
        else:
            ratio = new / rr
            curvature = rw + ratio * (rs + pw) + ratio * ratio * curvature
            p = r + ratio * p
            s = w + ratio * s
            if not last:
                z = q + ratio * z
        rr = new
        step = rr / curvature
        x = x + step * p
        r = r - step * s
        if not last:
            w = w - step * z
    charges_out[...] = x
    residual_out[...] = r

    for rnd in range(ITERS):
        wait_all(fields.at[rnd, SELF, 0], field_send.at[rnd, SELF])

        @pl.when(clu < owners - 1)
        def _():
            wait_all(fields.at[rnd, BELOW], field_send.at[rnd, BELOW])

        @pl.when(clu > 0)
        def _():
            wait_all(fields.at[rnd, ABOVE], field_send.at[rnd, ABOVE])

    for rnd in range(ITERS + 1):
        wait_all(inbox.at[rnd, pl.ds(0, peers)], slab_send.at[rnd])


def shards(
    electronegativity,
    mm_potential,
    hardness,
    near_blocks,
    near_source,
    basis_in,
    far_coupling,
    far_source,
    far_target,
    far_count,
):
    clusters, atoms = hardness.shape
    owners = far_coupling.shape[1]
    width = far_coupling.shape[2] * basis_in.shape[1]
    vmem = pl.BlockSpec(memory_space=pltpu.VMEM)
    smem = pl.BlockSpec(memory_space=pltpu.SMEM)
    whole = pl.BlockSpec(memory_space=pl.ANY)
    rounds = ITERS + 1
    return pl.pallas_call(
        functools.partial(kernel, owners),
        out_shape=(jax.ShapeDtypeStruct(hardness.shape, F32),) * 2,
        in_specs=[vmem, vmem, vmem, whole, vmem, vmem, vmem, smem, smem],
        out_specs=(vmem, vmem),
        scratch_shapes=[
            pltpu.VMEM(near_blocks.shape, BF16),
            pltpu.VMEM((owners * width, atoms), BF16),
            pltpu.VMEM((owners * width, 2 * atoms), BF16),
            pltpu.VMEM((owners, clusters, width), F32),
            pltpu.VMEM((ITERS, 3, 2, clusters, atoms), F32),
            pltpu.VMEM((rounds, owners, 8, 128), F32),
            pltpu.VMEM((rounds, 2 * owners, 8, 128), F32),
            pltpu.SemaphoreType.DMA,
            pltpu.SemaphoreType.DMA((ITERS, 3)),
            pltpu.SemaphoreType.DMA((ITERS, 3)),
            pltpu.SemaphoreType.DMA((rounds,)),
            pltpu.SemaphoreType.DMA((rounds,)),
        ],
        compiler_params=pltpu.CompilerParams(
            collective_id=0, has_side_effects=True, vmem_limit_bytes=50 * 2**20
        ),
    )(
        electronegativity,
        mm_potential,
        hardness,
        near_blocks,
        near_source,
        basis_in,
        far_coupling,
        far_target,
        far_count,
    )


def solution(mesh):
    placed = (
        P(("rep", "clu"), "sub"),
        P(("rep", "clu"), "sub"),
        P(("rep", "clu"), "sub"),
        P(("rep", "clu"), None, "sub", None),
        P(("rep", "clu"), None),
        P(("rep", "clu"), None, "sub"),
        P(("rep", "clu"), None, None, None),
        P(("rep", "clu"), None, None),
        P(("rep", "clu"), None, None),
        P(("rep", "clu"), None),
    )
    return jax.shard_map(
        shards,
        mesh=mesh,
        in_specs=placed,
        out_specs=(P(("rep", "clu"), "sub"), P(("rep", "clu"), "sub")),
        check_vma=False,
    )
```

time: 299 us -> 34.7 us (0.12)
  blocking collectives: 257 us -> 0 us
  Pallas kernels: 0 us -> 25.2 us
  starting transfers between devices: 11.1 us -> 0 us
  matrix products: 9.11 us -> 0 us
  other arithmetic: 7.74 us -> 0 us
  between operations: 7.56 us -> 0.65 us
    psum x8 -> x0, blocking collectives: 158 us -> none  [the longest x2 60.2 us: shards(): norm_next = lax.psum(jnp.sum(residual * residual), ('clu', 'sub'))]
    all_gather x6 -> x0, blocking collectives: 99.1 us -> none  [the longest x3 93.6 us: shards(): piece = lax.all_gather(apply_coeffs, 'clu', axis=0, tiled=True)]
    pallas_call x0 -> x1, Pallas kernels: none -> 25.2 us  [shards(): pl.pallas_call(functools.partial(kernel, owners), out_shape=(jax.ShapeDty...]
    ppermute x6 -> x0, starting transfers between devices: 11.1 us -> none  [the longest x3 7.24 us: with_halo(): before = lax.ppermute(last, axis, up)]
    dot_general x15 -> x0, matrix products: 9.11 us -> none  [the longest x3 3.95 us: shards(): jnp.einsum('cnab,cnb->ca', near_blocks.astype(jnp.float32), picked, preci...]
    unnamed x6 -> x18, local copies, waits for them, and re-layouts: 0.02 us -> 8.5 us
    reduce_sum x6 -> x0, other arithmetic: 4.51 us -> none  [the longest x3 1.87 us: shards(): curvature = lax.psum(jnp.sum(direction * product_vec), ('clu', 'sub'))]
    gather x9 -> x0, local copies, waits for them, and re-layouts: 3.53 us -> none  [the longest x6 1.81 us: shards(): picked = jnp.take(widened, near_local, axis=0)]
  transfers between devices with their start and end apart: 6 -> 0, of which waited for: 0 -> 0; matrix products, arithmetic and copies ran while one was open for 4% -> 0% of each run, Pallas kernels for 0% -> 0%
where the time goes in v1:
time: 34.7 us; the launch traced here: 34.3 us
  Pallas kernels  25.2 us (73%)
  local copies, waits for them, and re-layouts  8.5 us (24%)
  between operations  0.65 us (2%)
    pallas_call x1, Pallas kernels, shards(): pl.pallas_call(functools.partial(kernel, owners), out_shape=(jax.ShapeDty...  25.2 us
    unnamed x18, local copies, waits for them, and re-layouts  8.5 us

profile of v1, /device:TPU:0, one launch (start us, length us, event | category | flops | bytes accessed | tf_op | source)
XLA Modules:
  0.0 34.3 jit_solution(9130082256154602234)
XLA Ops:
  0.6 0.8 %copy.11.near_source = s32[8,3]{1,0:T(8,128)S(1)} copy(s32[8,3]{0,1:T(4,128)} %param.14) | data formatting | bytes 192 | tf_op args[4]
  1.4 0.8 %copy.12.target = s32[1,8,4]{2,1,0:T(8,128)S(1)} copy(s32[1,8,4]{1,2,0:T(4,128)} %param.17) | data formatting | bytes 256 | tf_op args[8]
  2.1 0.0 copy-start
  2.1 1.4 %copy-done = bf16[8,3,128,256]{3,2,1,0:T(8,128)(2,1)S(1)} copy-done((bf16[8,3,128,256]{3,2,1,0:T(8,128)(2,1)S(1)}, bf16[8,3,128,256]{3,2,1,0:T(8,128)(2,1)}, u32[]{:S(2)}) %copy-start) | copy-done | bytes 1572888
  3.6 0.0 copy-start.1
  3.6 0.8 %copy-done.1 = bf16[8,32,128]{2,1,0:T(8,128)(2,1)S(1)} copy-done((bf16[8,32,128]{2,1,0:T(8,128)(2,1)S(1)}, bf16[8,32,128]{2,1,0:T(8,128)(2,1)}, u32[]{:S(2)}) %copy-start.1) | copy-done | bytes 65560
  4.4 0.0 copy-start.2
  4.4 0.8 %copy-done.2 = bf16[1,8,4,1024]{3,2,1,0:T(4,128)(2,1)S(1)} copy-done((bf16[1,8,4,1024]{3,2,1,0:T(4,128)(2,1)S(1)}, bf16[1,8,4,1024]{3,2,1,0:T(4,128)(2,1)}, u32[]{:S(2)}) %copy-start.2) | copy-done | bytes 65560
  5.2 0.0 copy-start.3
  5.2 0.7 %copy-done.3 = f32[8,128]{1,0:T(8,128)S(1)} copy-done((f32[8,128]{1,0:T(8,128)S(1)}, f32[8,128]{1,0:T(8,128)}, u32[]{:S(2)}) %copy-start.3) | copy-done | bytes 4120
  5.9 0.0 copy-start.4
  5.9 0.7 %copy-done.4 = f32[8,128]{1,0:T(8,128)S(1)} copy-done((f32[8,128]{1,0:T(8,128)S(1)}, f32[8,128]{1,0:T(8,128)}, u32[]{:S(2)}) %copy-start.4) | copy-done | bytes 4120
  6.6 0.0 copy-start.5
  6.6 0.7 %copy-done.5 = f32[8,128]{1,0:T(8,128)S(1)} copy-done((f32[8,128]{1,0:T(8,128)S(1)}, f32[8,128]{1,0:T(8,128)}, u32[]{:S(2)}) %copy-start.5) | copy-done | bytes 4120
  7.3 0.0 copy-start.6
  7.3 0.7 %copy-done.6 = s32[1,8]{1,0:T(1,128)S(1)} copy-done((s32[1,8]{1,0:T(1,128)S(1)}, s32[1,8]{1,0:T(1,128)}, u32[]{:S(2)}) %copy-start.6) | copy-done | bytes 56
  7.9 25.2 %shard_map.104 = (f32[8,128]{1,0:T(8,128)S(1)}, f32[8,128]{1,0:T(8,128)S(1)}) custom-call(f32[8,128]{1,0:T(8,128)S(1)} %copy-done.3, f32[8,128]{1,0:T(8,128)S(1)} %copy-done.4, f32[8,128]{1,0:T(8,128)S(1)} %copy-done.5, bf16[8,3,128,256]{3,2,1,0:T(8,128)(2,1)S(1)} %copy-done, s32[8,3]{1,0:T(8,128)S(1)} %copy.11.near_source, ...), custom_call_target="tpu_custom_call" | custom-call | tf_op jit(solution)/shard_map/pallas_call | solution.py:371
  33.1 0.6 %copy.15 = f32[8,128]{1,0:T(8,128)} copy(f32[8,128]{1,0:T(8,128)S(1)} %get-tuple-element.4) | data formatting | bytes 8192
  33.7 0.6 %copy.16 = f32[8,128]{1,0:T(8,128)} copy(f32[8,128]{1,0:T(8,128)S(1)} %get-tuple-element.5) | data formatting | bytes 8192
Async XLA Ops:
  2.1 1.4 %copy-start = (bf16[8,3,128,256]{3,2,1,0:T(8,128)(2,1)S(1)}, bf16[8,3,128,256]{3,2,1,0:T(8,128)(2,1)}, u32[]{:S(2)}) copy-start(bf16[8,3,128,256]{3,2,1,0:T(8,128)(2,1)} %near_hbm.1) | copy-start | bytes 4718596
  3.6 0.8 %copy-start.1 = (bf16[8,32,128]{2,1,0:T(8,128)(2,1)S(1)}, bf16[8,32,128]{2,1,0:T(8,128)(2,1)}, u32[]{:S(2)}) copy-start(bf16[8,32,128]{2,1,0:T(8,128)(2,1)} %basis.1) | copy-start | bytes 196612
  4.4 0.8 %copy-start.2 = (bf16[1,8,4,1024]{3,2,1,0:T(4,128)(2,1)S(1)}, bf16[1,8,4,1024]{3,2,1,0:T(4,128)(2,1)}, u32[]{:S(2)}) copy-start(bf16[1,8,4,1024]{3,2,1,0:T(4,128)(2,1)} %coupling.1) | copy-start | bytes 196612
  5.2 0.7 %copy-start.3 = (f32[8,128]{1,0:T(8,128)S(1)}, f32[8,128]{1,0:T(8,128)}, u32[]{:S(2)}) copy-start(f32[8,128]{1,0:T(8,128)} %electro.1) | copy-start | bytes 12292
  5.9 0.7 %copy-start.4 = (f32[8,128]{1,0:T(8,128)S(1)}, f32[8,128]{1,0:T(8,128)}, u32[]{:S(2)}) copy-start(f32[8,128]{1,0:T(8,128)} %potential.1) | copy-start | bytes 12292
  6.6 0.7 %copy-start.5 = (f32[8,128]{1,0:T(8,128)S(1)}, f32[8,128]{1,0:T(8,128)}, u32[]{:S(2)}) copy-start(f32[8,128]{1,0:T(8,128)} %hardness_ref.1) | copy-start | bytes 12292
  7.3 0.7 %copy-start.6 = (s32[1,8]{1,0:T(1,128)S(1)}, s32[1,8]{1,0:T(1,128)}, u32[]{:S(2)}) copy-start(s32[1,8]{1,0:T(1,128)} %count.1) | copy-start | bytes 100

commit v2 on v1

--- a/solution.py
+++ b/solution.py
@@ -34,32 +34,31 @@
 
 def kernel(
     owners,
-    electro,
-    potential,
-    hardness_ref,
-    near_hbm,
-    near_source,
-    basis,
-    coupling,
-    target,
-    count,
-    charges_out,
-    residual_out,
-    near,
-    picked_basis,
-    expand,
-    mask,
-    fields,
-    outbox,
-    inbox,
-    load_sem,
-    field_send,
-    field_recv,
-    slab_send,
-    slab_recv,
+    *refs,
 ):
+    arguments, refs = (refs[:9], refs[9:])
+    charges_out, residual_out = refs[:2]
+    held, refs = (refs[2:11], refs[11:])
+    target, count, basis, electro, potential, coupling, near, near_source, hardness_ref = held
+    (
+        picked_basis,
+        expand,
+        mask,
+        fields,
+        outbox,
+        inbox,
+        load_sem,
+        field_send,
+        field_recv,
+        slab_send,
+        slab_recv,
+    ) = refs
+    loads = [
+        pltpu.make_async_copy(source, place, load_sem.at[i])
+        for i, (source, place) in enumerate(zip(arguments, held))
+    ]
     clusters, atoms = hardness_ref.shape
-    slots = target.shape[2]
+    slots = target.shape[1]
     rank = basis.shape[1]
     width = slots * rank
     group = 8
@@ -79,14 +78,14 @@
         act(clu, 1 - sub)
         each(1, owners, owner_step)
 
+    for copy in loads:
+        copy.start()
     barrier = pltpu.get_barrier_semaphore()
     to_peers(
         lambda d, t: pl.semaphore_signal(
             barrier, inc=1, device_id={"clu": d, "sub": t}, device_id_type=MESH
         )
     )
-    load = pltpu.make_async_copy(near_hbm, near, load_sem)
-    load.start()
 
     row8 = lax.broadcasted_iota(jnp.int32, (clusters, 128), 0)
     slot_of_lane = lax.broadcasted_iota(jnp.int32, (clusters, width), 1) // rank
@@ -94,7 +93,7 @@
     def prepare(s):
         wanted = jnp.full((clusters, width), -1, jnp.int32)
         for k in range(slots):
-            t = target[0, s, k]
+            t = target[0, k, s]
             picked_basis[pl.ds((s * slots + k) * rank, rank), :] = basis[t]
             wanted = jnp.where(slot_of_lane == k, t, wanted)
         hit = (wanted == lax.broadcasted_iota(jnp.int32, (clusters, width), 0)) & (
@@ -102,6 +101,8 @@
         )
         mask[s] = jnp.where(hit, 1.0, 0.0)
 
+    for copy in loads[:3]:
+        copy.wait()
     each(0, owners, prepare)
 
     def send_field(rnd, v):
@@ -182,13 +183,12 @@
             return jnp.concatenate([fields[rnd, kind, 0], fields[rnd, kind, 1]], axis=1)
 
         own, above, below = (whole(SELF), whole(ABOVE), whole(BELOW))
-        here = clu * clusters + lax.broadcasted_iota(jnp.int32, (clusters, 1), 0)
         inputs = []
         for n in range(near.shape[1]):
             if n == 0:
                 value = own
             else:
-                origin = near_source[:, n : n + 1]
+                origin = origins[n]
                 value = jnp.where(
                     origin == here + clusters,
                     above,
@@ -281,7 +281,8 @@
 
         each(0, owners, step)
 
-    hardness = hardness_ref[...]
+    for copy in loads[3:5]:
+        copy.wait()
     r = -(electro[...] + potential[...])
     x = jnp.zeros_like(r)
     empty = jnp.zeros((8, 128), F32)
@@ -289,8 +290,18 @@
 
     send_field(0, r)
     send_far(0, r, empty)
+    loads[5].wait()
     build_expand()
-    load.wait()
+    for copy in loads[6:]:
+        copy.wait()
+    hardness = hardness_ref[...]
+    here = clu * clusters + lax.broadcasted_iota(jnp.int32, (clusters, 2 * atoms), 0)
+    origins = []
+    for n in range(near.shape[1]):
+        origin = here
+        for c in range(clusters):
+            origin = jnp.where(here == clu * clusters + c, near_source[n, c], origin)
+        origins.append(origin)
     w = hardness * r + near_term(0)
     receive(0)
     w = w + far_term(0)
@@ -365,42 +376,47 @@
     owners = far_coupling.shape[1]
     width = far_coupling.shape[2] * basis_in.shape[1]
     vmem = pl.BlockSpec(memory_space=pltpu.VMEM)
-    smem = pl.BlockSpec(memory_space=pltpu.SMEM)
-    whole = pl.BlockSpec(memory_space=pl.ANY)
+    hbm = pl.BlockSpec(memory_space=pltpu.HBM)
     rounds = ITERS + 1
+    arguments = (
+        jnp.swapaxes(far_target, 1, 2),
+        far_count,
+        basis_in,
+        electronegativity,
+        mm_potential,
+        far_coupling,
+        near_blocks,
+        jnp.swapaxes(near_source, 0, 1),
+        hardness,
+    )
+    scalars = (0, 1, 7)
+    held = [
+        (pltpu.SMEM if i in scalars else pltpu.VMEM)(a.shape, a.dtype)
+        for i, a in enumerate(arguments)
+    ]
     return pl.pallas_call(
         functools.partial(kernel, owners),
         out_shape=(jax.ShapeDtypeStruct(hardness.shape, F32),) * 2,
-        in_specs=[vmem, vmem, vmem, whole, vmem, vmem, vmem, smem, smem],
+        in_specs=[hbm] * len(arguments),
         out_specs=(vmem, vmem),
-        scratch_shapes=[
-            pltpu.VMEM(near_blocks.shape, BF16),
+        scratch_shapes=held
+        + [
             pltpu.VMEM((owners * width, atoms), BF16),
             pltpu.VMEM((owners * width, 2 * atoms), BF16),
             pltpu.VMEM((owners, clusters, width), F32),
             pltpu.VMEM((ITERS, 3, 2, clusters, atoms), F32),
             pltpu.VMEM((rounds, owners, 8, 128), F32),
             pltpu.VMEM((rounds, 2 * owners, 8, 128), F32),
-            pltpu.SemaphoreType.DMA,
+            pltpu.SemaphoreType.DMA((len(arguments),)),
             pltpu.SemaphoreType.DMA((ITERS, 3)),
             pltpu.SemaphoreType.DMA((ITERS, 3)),
             pltpu.SemaphoreType.DMA((rounds,)),
             pltpu.SemaphoreType.DMA((rounds,)),
         ],
         compiler_params=pltpu.CompilerParams(
-            collective_id=0, has_side_effects=True, vmem_limit_bytes=50 * 2**20
+            collective_id=0, has_side_effects=True, vmem_limit_bytes=64 * 2**20
         ),
-    )(
-        electronegativity,
-        mm_potential,
-        hardness,
-        near_blocks,
-        near_source,
-        basis_in,
-        far_coupling,
-        far_target,
-        far_count,
-    )
+    )(*arguments)
 
 
 def solution(mesh):

time: 34.7 us -> 28.7 us (0.83)
  local copies, waits for them, and re-layouts: 8.5 us -> 2.53 us
    unnamed x18 -> x2, local copies, waits for them, and re-layouts: 8.5 us -> 2.53 us
where the time goes in v2:
time: 28.7 us; the launch traced here: 28.5 us
  Pallas kernels  25.3 us (88%)
  local copies, waits for them, and re-layouts  2.53 us (9%)
  between operations  0.64 us (2%)
    pallas_call x1, Pallas kernels, shards(): pl.pallas_call(functools.partial(kernel, owners), out_shape=(jax.ShapeDty...  25.3 us
    unnamed x2, local copies, waits for them, and re-layouts  2.53 us

profile of v2, /device:TPU:0, one launch (start us, length us, event | category | flops | bytes accessed | tf_op | source)
XLA Modules:
  0.0 28.5 jit_solution(7201798932796614918)
XLA Ops:
  0.6 25.3 %shard_map.104 = (f32[8,128]{1,0:T(8,128)}, f32[8,128]{1,0:T(8,128)}) custom-call(s32[1,4,8]{2,1,0:T(4,128)} %bitcast.2, s32[1,8]{1,0:T(1,128)} %refs_1_.1, bf16[8,32,128]{2,1,0:T(8,128)(2,1)} %refs_2_.1, f32[8,128]{1,0:T(8,128)} %refs_3_.1, f32[8,128]{1,0:T(8,128)} %refs_4_.1, bf16[1,8,4,1024]{3,2,1,0:T(4,128)(2,1)} %refs_5_.1, ...), custom_call_target="tpu_custom_call" | custom-call | tf_op jit(solution)/shard_map/pallas_call | solution.py:397
  25.9 1.3 %copy.13 = f32[8,128]{1,0:T(8,128)} copy(f32[8,128]{1,0:T(8,128)} %get-tuple-element.4) | data formatting | bytes 8192
  27.2 1.3 %copy.14 = f32[8,128]{1,0:T(8,128)} copy(f32[8,128]{1,0:T(8,128)} %get-tuple-element.5) | data formatting | bytes 8192

commit v3 on v2

--- a/solution.py
+++ b/solution.py
@@ -37,8 +37,8 @@
     *refs,
 ):
     arguments, refs = (refs[:9], refs[9:])
-    charges_out, residual_out = refs[:2]
-    held, refs = (refs[2:11], refs[11:])
+    results = refs[0]
+    held, refs = (refs[1:10], refs[10:])
     target, count, basis, electro, potential, coupling, near, near_source, hardness_ref = held
     (
         picked_basis,
@@ -78,14 +78,15 @@
         act(clu, 1 - sub)
         each(1, owners, owner_step)
 
-    for copy in loads:
-        copy.start()
     barrier = pltpu.get_barrier_semaphore()
     to_peers(
         lambda d, t: pl.semaphore_signal(
             barrier, inc=1, device_id={"clu": d, "sub": t}, device_id_type=MESH
         )
     )
+
+    for copy in loads:
+        copy.start()
 
     row8 = lax.broadcasted_iota(jnp.int32, (clusters, 128), 0)
     slot_of_lane = lax.broadcasted_iota(jnp.int32, (clusters, width), 1) // rank
@@ -145,7 +146,7 @@
         to_peers(copy)
         inbox[rnd, mine] = sums
 
-    def send_far(rnd, v, sums):
+    def fill_far(rnd, v, sums):
         parts = jnp.concatenate(halves(v), axis=0)
 
         def group_step(g):
@@ -159,7 +160,6 @@
                 outbox[rnd, g * group + j] = jnp.where(row8 == 0, line, sums)
 
         each(0, groups, group_step)
-        send_slabs(rnd, jnp.where(row8 == 0, 0.0, sums))
 
     def send_sums(rnd, sums):
         each(0, owners, lambda d: outbox.__setitem__((rnd, d), sums))
@@ -169,46 +169,45 @@
         pltpu.make_async_copy(ref, ref, sem).wait()
 
     def near_term(rnd):
-        wait_all(fields.at[rnd, SELF, 0], field_recv.at[rnd, SELF])
-
-        @pl.when(clu < owners - 1)
-        def _():
-            wait_all(fields.at[rnd, ABOVE], field_recv.at[rnd, ABOVE])
-
-        @pl.when(clu > 0)
-        def _():
-            wait_all(fields.at[rnd, BELOW], field_recv.at[rnd, BELOW])
-
         def whole(kind):
             return jnp.concatenate([fields[rnd, kind, 0], fields[rnd, kind, 1]], axis=1)
 
-        own, above, below = (whole(SELF), whole(ABOVE), whole(BELOW))
-        inputs = []
-        for n in range(near.shape[1]):
-            if n == 0:
-                value = own
-            else:
-                origin = origins[n]
-                value = jnp.where(
-                    origin == here + clusters,
-                    above,
-                    jnp.where(origin == here - clusters, below, own),
-                )
+        def masked(value, c):
+            return jnp.where(owner_row == c, value, jnp.zeros_like(value))
+
+        def apply(total, inputs, blocks):
+            for first, second in zip(blocks[::2], blocks[1::2]):
+                left = jnp.concatenate([masked(inputs[n], c) for c, n in (first, second)], axis=0)
+                right = jnp.concatenate([near[c, n] for c, n in (first, second)], axis=0)
+                product = contract(left, right, ((1,), (1,)))
+                total = product if total is None else total + product
+            return total
+
+        wait_all(fields.at[rnd, SELF, 0], field_recv.at[rnd, SELF])
+        own = whole(SELF)
+        inputs = [jnp.concatenate(halves(own), axis=0)]
+        owner_row = lax.broadcasted_iota(jnp.int32, inputs[0].shape, 0) % clusters
+        total = apply(None, inputs, [(c, 0) for c in range(clusters)])
+
+        @pl.when(clu < owners - 1)
+        def _():
+            wait_all(fields.at[rnd, ABOVE], field_recv.at[rnd, ABOVE])
+
+        @pl.when(clu > 0)
+        def _():
+            wait_all(fields.at[rnd, BELOW], field_recv.at[rnd, BELOW])
+
+        above, below = (whole(ABOVE), whole(BELOW))
+        for n in range(1, near.shape[1]):
+            origin = origins[n]
+            value = jnp.where(
+                origin == here + clusters,
+                above,
+                jnp.where(origin == here - clusters, below, own),
+            )
             inputs.append(jnp.concatenate(halves(value), axis=0))
-        owner_row = lax.broadcasted_iota(jnp.int32, inputs[0].shape, 0) % clusters
-        total = None
-        blocks = [(c, n) for c in range(clusters) for n in range(near.shape[1])]
-        for first, second in zip(blocks[::2], blocks[1::2]):
-            left = jnp.concatenate(
-                [
-                    jnp.where(owner_row == c, inputs[n], jnp.zeros_like(inputs[n]))
-                    for c, n in (first, second)
-                ],
-                axis=0,
-            )
-            right = jnp.concatenate([near[c, n] for c, n in (first, second)], axis=0)
-            product = contract(left, right, ((1,), (1,)))
-            total = product if total is None else total + product
+        rest = [(c, n) for c in range(clusters) for n in range(1, near.shape[1])]
+        total = apply(total, inputs, rest)
         size = 2 * clusters
         first, second = (total[:size, :atoms], total[size:, atoms:])
         both = first + second
@@ -286,10 +285,10 @@
     r = -(electro[...] + potential[...])
     x = jnp.zeros_like(r)
     empty = jnp.zeros((8, 128), F32)
+    fill_far(0, r, empty)
     pl.semaphore_wait(barrier, peers)
-
+    send_slabs(0, empty)
     send_field(0, r)
-    send_far(0, r, empty)
     loads[5].wait()
     build_expand()
     for copy in loads[6:]:
@@ -318,8 +317,9 @@
             send_sums(rnd, sums)
             receive(rnd)
         else:
+            fill_far(rnd, w, sums)
+            send_slabs(rnd, jnp.where(row8 == 0, 0.0, sums))
             send_field(rnd, w)
-            send_far(rnd, w, sums)
             q = hardness * w + near_term(rnd)
             receive(rnd)
         new, rw, rs, pw = totals(rnd)
@@ -342,8 +342,8 @@
         r = r - step * s
         if not last:
             w = w - step * z
-    charges_out[...] = x
-    residual_out[...] = r
+    results[0] = x
+    results[1] = r
 
     for rnd in range(ITERS):
         wait_all(fields.at[rnd, SELF, 0], field_send.at[rnd, SELF])
@@ -394,11 +394,11 @@
         (pltpu.SMEM if i in scalars else pltpu.VMEM)(a.shape, a.dtype)
         for i, a in enumerate(arguments)
     ]
-    return pl.pallas_call(
+    both = pl.pallas_call(
         functools.partial(kernel, owners),
-        out_shape=(jax.ShapeDtypeStruct(hardness.shape, F32),) * 2,
+        out_shape=jax.ShapeDtypeStruct((2,) + hardness.shape, F32),
         in_specs=[hbm] * len(arguments),
-        out_specs=(vmem, vmem),
+        out_specs=vmem,
         scratch_shapes=held
         + [
             pltpu.VMEM((owners * width, atoms), BF16),
@@ -417,6 +417,7 @@
             collective_id=0, has_side_effects=True, vmem_limit_bytes=64 * 2**20
         ),
     )(*arguments)
+    return (both[0], both[1])
 
 
 def solution(mesh):

time: 28.7 us -> 27.1 us (0.944)
  local copies, waits for them, and re-layouts: 2.53 us -> 1.28 us
  Pallas kernels: 25.3 us -> 25 us
    unnamed x2 -> x0, local copies, waits for them, and re-layouts: 2.53 us -> none
    squeeze x0 -> x1, local copies, waits for them, and re-layouts: none -> 1.28 us  [shards(): return (both[0], both[1])]
    pallas_call x1, Pallas kernels: 25.3 us -> 25 us  [shards(): pl.pallas_call(functools.partial(kernel, owners), out_shape=jax.ShapeDtyp...]
where the time goes in v3:
time: 27.1 us; the launch traced here: 26.9 us
  Pallas kernels  25 us (92%)
  local copies, waits for them, and re-layouts  1.28 us (5%)
  between operations  0.64 us (2%)
    pallas_call x1, Pallas kernels, shards(): pl.pallas_call(functools.partial(kernel, owners), out_shape=jax.ShapeDtyp...  25 us
    squeeze x1, local copies, waits for them, and re-layouts, shards(): return (both[0], both[1])  1.28 us

profile of v3, /device:TPU:0, one launch (start us, length us, event | category | flops | bytes accessed | tf_op | source)
XLA Modules:
  0.0 26.9 jit_solution(11291896255630929922)
XLA Ops:
  0.6 25.0 %shard_map.104 = f32[2,8,128]{2,1,0:T(8,128)} custom-call(s32[1,4,8]{2,1,0:T(4,128)} %bitcast.6, s32[1,8]{1,0:T(1,128)} %refs_1_.1, bf16[8,32,128]{2,1,0:T(8,128)(2,1)} %refs_2_.1, f32[8,128]{1,0:T(8,128)} %refs_3_.1, f32[8,128]{1,0:T(8,128)} %refs_4_.1, bf16[1,8,4,1024]{3,2,1,0:T(4,128)(2,1)} %refs_5_.1, bf16[8,3,128,256]{3,2,1,0:T(8,128)(2,1)} %refs_6_.1, ...), custom_call_target="tpu_custom_call" | custom-call | tf_op jit(solution)/shard_map/pallas_call | solution.py:397
  25.6 1.3 %slice_bitcast_fusion = (f32[8,128]{1,0:T(8,128)}, f32[8,128]{1,0:T(8,128)}) fusion(f32[2,8,128]{2,1,0:T(8,128)} %shard_map.104), kind=kLoop, calls=%fused_computation | loop fusion | bytes 16384 | tf_op jit(solution)/shard_map/squeeze | solution.py:420

commit v4 on v3

--- a/solution.py
+++ b/solution.py
@@ -70,13 +70,18 @@
     mine = 2 * clu + sub
 
     def to_peers(act):
-        def owner_step(o):
-            d = lax.rem(clu + o, owners)
+        upper = lax.div(clu, owners // 2)
+
+        def owner_step(i):
+            rising = i + lax.div(i - clu + owners, owners)
+            falling = owners - 1 - i
+            falling = falling - lax.div(clu - falling + owners, owners)
+            d = upper * rising + (1 - upper) * falling
             act(d, 0)
             act(d, 1)
 
+        each(0, owners - 1, owner_step)
         act(clu, 1 - sub)
-        each(1, owners, owner_step)
 
     barrier = pltpu.get_barrier_semaphore()
     to_peers(

time: 27.1 us -> 26.5 us (0.978)
  Pallas kernels: 25 us -> 24.4 us
    pallas_call x1, Pallas kernels: 25 us -> 24.4 us  [shards(): pl.pallas_call(functools.partial(kernel, owners), out_shape=jax.ShapeDtyp...]
where the time goes in v4:
time: 26.5 us; the launch traced here: 26.3 us
  Pallas kernels  24.4 us (92%)
  local copies, waits for them, and re-layouts  1.28 us (5%)
  between operations  0.64 us (2%)
    pallas_call x1, Pallas kernels, shards(): pl.pallas_call(functools.partial(kernel, owners), out_shape=jax.ShapeDtyp...  24.4 us
    squeeze x1, local copies, waits for them, and re-layouts, shards(): return (both[0], both[1])  1.28 us

profile of v4, /device:TPU:0, one launch (start us, length us, event | category | flops | bytes accessed | tf_op | source)
XLA Modules:
  0.0 26.3 jit_solution(12445350587338257575)
XLA Ops:
  0.6 24.4 %shard_map.104 = f32[2,8,128]{2,1,0:T(8,128)} custom-call(s32[1,4,8]{2,1,0:T(4,128)} %bitcast.6, s32[1,8]{1,0:T(1,128)} %refs_1_.1, bf16[8,32,128]{2,1,0:T(8,128)(2,1)} %refs_2_.1, f32[8,128]{1,0:T(8,128)} %refs_3_.1, f32[8,128]{1,0:T(8,128)} %refs_4_.1, bf16[1,8,4,1024]{3,2,1,0:T(4,128)(2,1)} %refs_5_.1, bf16[8,3,128,256]{3,2,1,0:T(8,128)(2,1)} %refs_6_.1, ...), custom_call_target="tpu_custom_call" | custom-call | tf_op jit(solution)/shard_map/pallas_call | solution.py:402
  25.0 1.3 %slice_bitcast_fusion = (f32[8,128]{1,0:T(8,128)}, f32[8,128]{1,0:T(8,128)}) fusion(f32[2,8,128]{2,1,0:T(8,128)} %shard_map.104), kind=kLoop, calls=%fused_computation | loop fusion | bytes 16384 | tf_op jit(solution)/shard_map/squeeze | solution.py:425
